TPU v7x, 512 devices: a whole 4x4x16 slice. The times are simulated.
512 devices in a mesh: blk: 128 (over z, y, core), grp: 4 (over x).
Axes of the slice: x: 4, y: 4, z: 16, core: 2. Of those that a mesh axis runs over, the one named last changes fastest.
Arguments:
- jac_tiles: float32 [32768, 128, 128], P(('blk', 'grp')), may hold values from -0.125 to 0.125
- tile_row: int32 [32768], P(('blk', 'grp')), may hold values from 0 to 3
- tile_slot: int32 [32768], P(('blk', 'grp')), may hold values from 0 to 127, as said below
- send_list: int32 [65536], P(('blk', 'grp')), may hold values from 0 to 7
- ray_counts: int32 [2048], P(('blk', 'grp')), may hold values from 32 to 128
- travel_times: float32 [262144], P(('blk', 'grp')), may hold values from -40 to 40
Outputs:
- solution: float32 [131072], P('blk')
- ray_dir: float32 [262144], P(('blk', 'grp'))
Inputs may be any that keep to these rules, and one draw needn't show every extreme that they name: `tile_slot`: the 64 tiles of one device name 64 different owners.
All inputs are finite; a program needn't handle non-finite values.
Results may differ from a plain program's by a relative error of at most 0.0003.
Values sent between devices are 32-bit elements; how exact they have to be, the bound alone decides.
A program may use at most 64 MiB of HBM per device.

v0:
```python
import jax
import jax.numpy as jnp
from jax import lax
from jax.sharding import PartitionSpec as P

CPD = 8
ITERS = 2


epsilon = 1e-06


def mat(left, right):
    return jnp.dot(left, right, precision=lax.Precision.HIGHEST, preferred_element_type=jnp.float32)


def ray_length(vector):
    return jnp.sqrt(lax.psum(jnp.sum(vector * vector), ("blk", "grp")) + epsilon)


def cell_length(vector):
    return jnp.sqrt(lax.psum(jnp.sum(vector * vector), "blk") + epsilon)


def body(jac_tiles, tile_row, tile_slot, send_list, ray_counts, travel_times):
    tile_size = jac_tiles.shape[1]
    row_blocks = ray_counts.shape[0]
    blk_count = lax.axis_size("blk")
    highest = lax.Precision.HIGHEST
    live_rows = (jnp.arange(tile_size, dtype=jnp.int32)[None, :] < ray_counts[:, None]).astype(
        jnp.float32
    )
    row_onehot = (tile_row[None, :] == jnp.arange(row_blocks, dtype=jnp.int32)[:, None]).astype(
        jnp.float32
    )
    slot_onehot = (tile_slot[:, None] == jnp.arange(blk_count, dtype=jnp.int32)[None, :]).astype(
        jnp.float32
    )
    fetched = lax.all_to_all(
        send_list.reshape(blk_count, 1), "blk", split_axis=0, concat_axis=0, tiled=True
    )
    glob_cols = tile_slot * CPD + jnp.sum(
        slot_onehot.astype(jnp.int32) * fetched[:, 0][None, :], axis=1
    )
    glob_onehot = (
        glob_cols[:, None] == jnp.arange(blk_count * CPD, dtype=jnp.int32)[None, :]
    ).astype(jnp.float32)

    def transpose(ray_vec):
        spread = mat(row_onehot.T, ray_vec)
        partial_value = jnp.einsum("kij,ki->kj", jac_tiles, spread, precision=highest)
        all_cells = mat(glob_onehot.T, partial_value)
        owned = lax.psum_scatter(all_cells, "blk", scatter_dimension=0, tiled=True)
        return lax.psum(owned, "grp")

    data = travel_times.reshape(row_blocks, tile_size) * live_rows
    zero_cells = jnp.zeros((CPD, tile_size), jnp.float32)
    beta_norm = ray_length(data)
    ray_dir = data / beta_norm
    cell_res = transpose(ray_dir)
    alpha_norm = cell_length(cell_res)
    model_dir = cell_res / alpha_norm
    search_dir = model_dir
    solution = zero_cells
    phi_bar = beta_norm
    rho_bar = alpha_norm
    for iteration in range(ITERS):
        model_all = lax.all_gather(model_dir, "blk", axis=0, tiled=True)
        picked = mat(glob_onehot, model_all)
        products = jnp.einsum("kij,kj->ki", jac_tiles, picked, precision=highest)
        ray_res = mat(row_onehot, products) * live_rows - alpha_norm * ray_dir
        beta_norm = ray_length(ray_res)
        ray_dir = ray_res / beta_norm
        cell_res = transpose(ray_dir) - beta_norm * model_dir
        alpha_norm = cell_length(cell_res)
        model_dir = cell_res / alpha_norm
        rho_now = jnp.sqrt(rho_bar * rho_bar + beta_norm * beta_norm)
        cosine = rho_bar / rho_now
        sine_val = beta_norm / rho_now
        theta_now = sine_val * alpha_norm
        rho_bar = -cosine * alpha_norm
        phi_now = cosine * phi_bar
        phi_bar = sine_val * phi_bar
        solution = solution + phi_now / rho_now * search_dir
        search_dir = model_dir - theta_now / rho_now * search_dir
    return (solution.reshape(-1), ray_dir.reshape(-1))


def solution(mesh):
    in_specs = (
        P(("blk", "grp"), None, None),
        P(("blk", "grp")),
        P(("blk", "grp")),
        P(("blk", "grp")),
        P(("blk", "grp")),
        P(("blk", "grp")),
    )
    out_specs = (P("blk"), P(("blk", "grp")))
    return jax.shard_map(body, mesh=mesh, in_specs=in_specs, out_specs=out_specs, check_vma=False)
```

profile of v0, /device:TPU:1, one launch (start us, length us, event | category | flops | bytes accessed | tf_op | source)
XLA Modules:
  0.0 1717.8 jit_solution(2084933794279917194)
XLA Ops:
  7.2 0.0 copy-start.3
  7.2 1.4 copy.10
  8.6 1.4 multiply_reduce_fusion.5
  9.9 20.6 %all-to-all-start = ((s32[128,1,1]{2,1,0:T(1,128)}), s32[128,1,1]{2,1,0:T(1,128)S(1)}, u32[]{:S(2)}, u32[]{:S(2)}) async-start(s32[128,1,1]{2,1,0:T(1,128)} %copy.10), calls=%async_computation | async-start | bytes 131072 | tf_op jit(solution)/shard_map/all_to_all | solution.py:39
  30.5 0.0 all-reduce.5.cloned.1.call-start
  30.5 105.8 %psum.49 = f32[]{:T(128)} all-reduce(f32[]{:T(128)} %multiply_reduce_fusion.5), channel_id=1, replica_groups=mesh['blk'=128,'grp'=4] {'blk','grp'}, use_global_device_ids=true, to_apply=%region_2.0 | all-reduce | flops 1 | bytes 8 | tf_op jit(solution)/shard_map/psum | solution.py:18
  137.0 0.9 fusion.13
  138.0 5.3 fusion.20
  143.2 0.0 copy-start
  143.2 0.0 copy-start.1
  143.2 0.0 copy-start.2
  143.2 0.0 all-to-all-done
  143.3 2.4 reduce.1
  145.6 0.0 copy-done.3
  145.6 0.2 multiply_reduce_fusion
  145.8 1.5 fusion.5
  147.3 0.0 all-reduce.5.cloned.1.call-update
  147.3 0.0 all-reduce.7.cloned.1.call-start
  147.4 1.3 dynamic-slice
  149.3 322.5 %all-reduce.5.cloned.1.call-done = f32[1024,128]{1,0:T(8,128)} async-done(((f32[1024,128]{1,0:T(8,128)}), f32[1024,128]{1,0:T(8,128)}) %all-reduce.5.cloned.1.call-update) | async-done | bytes 524304
  471.8 0.7 constant_dynamic-slice_fusion.1
  472.5 8.4 psum.50
  480.8 0.6 multiply_reduce_fusion.2
  481.4 250.4 %psum.51 = f32[]{:T(128)} all-reduce(f32[]{:T(128)} %multiply_reduce_fusion.2), channel_id=1, replica_groups=mesh['blk'=128,'grp'=4] {'blk'}, use_global_device_ids=true, to_apply=%region_6.0 | all-reduce | flops 1 | bytes 8 | tf_op jit(solution)/shard_map/psum | solution.py:22
  732.6 80.5 %all_gather.6 = f32[1024,128]{1,0:T(8,128)S(1)} all-gather(f32[8,128]{1,0:T(8,128)S(1)} %broadcast_divide_fusion.1), channel_id=1, replica_groups=mesh['blk'=128,'grp'=4] {'blk'}, dimensions={0}, use_global_device_ids=true | all-gather | bytes 528384 | tf_op jit(solution)/shard_map/all_gather | solution.py:68
  813.1 0.3 fusion.4
  813.4 8.3 fusion.21
  821.7 0.0 copy-done
  821.7 0.0 copy-done.1
  821.7 0.0 copy-done.2
  821.7 0.7 multiply_reduce_fusion.4
  822.5 101.9 %psum.52 = f32[]{:T(128)} all-reduce(f32[]{:T(128)} %get-tuple-element.2), channel_id=1, replica_groups=mesh['blk'=128,'grp'=4] {'blk','grp'}, use_global_device_ids=true, to_apply=%region_8.0 | all-reduce | flops 1 | bytes 8 | tf_op jit(solution)/shard_map/psum | solution.py:18
  925.1 0.2 fusion.12
  925.3 5.3 fusion.22
  930.6 1.5 fusion.3
  932.1 0.0 all-reduce.7.cloned.1.call-update
  932.3 324.0 %all-reduce.7.cloned.1.call-done = f32[1024,128]{1,0:T(8,128)} async-done(((f32[1024,128]{1,0:T(8,128)}), f32[1024,128]{1,0:T(8,128)}) %all-reduce.7.cloned.1.call-update) | async-done | bytes 524304
  1256.3 0.7 constant_dynamic-slice_fusion
  1257.0 8.4 psum.53
  1265.3 0.6 multiply_reduce_fusion.1
  1266.0 250.4 %psum.54 = f32[]{:T(128)} all-reduce(f32[]{:T(128)} %multiply_reduce_fusion.1), channel_id=1, replica_groups=mesh['blk'=128,'grp'=4] {'blk'}, use_global_device_ids=true, to_apply=%region_12.0 | all-reduce | flops 1 | bytes 8 | tf_op jit(solution)/shard_map/psum | solution.py:22
  1517.1 80.5 %all_gather.7 = f32[1024,128]{1,0:T(8,128)S(1)} all-gather(f32[8,128]{1,0:T(8,128)S(1)} %broadcast_divide_fusion), channel_id=1, replica_groups=mesh['blk'=128,'grp'=4] {'blk'}, dimensions={0}, use_global_device_ids=true | all-gather | bytes 528384 | tf_op jit(solution)/shard_map/all_gather | solution.py:68
  1597.6 0.3 fusion.2
  1598.0 8.3 fusion.23
  1606.3 0.8 multiply_reduce_fusion.3
  1607.0 101.9 %psum.55 = f32[]{:T(128)} all-reduce(f32[]{:T(128)} %get-tuple-element.4), channel_id=1, replica_groups=mesh['blk'=128,'grp'=4] {'blk','grp'}, use_global_device_ids=true, to_apply=%region_14.0 | all-reduce | flops 1 | bytes 8 | tf_op jit(solution)/shard_map/psum | solution.py:18
  1709.6 0.6 divide_bitcast_fusion
  1710.4 0.6 add_bitcast_fusion
  (3 shorter events, 0.0 us)
Async XLA Ops:
  7.2 138.4 %copy-start.3 = (s32[64]{0:T(128)S(1)}, s32[64]{0:T(128)}, u32[]{:S(2)}) copy-start(s32[64]{0:T(128)} %param.8) | copy-start | bytes 772
  9.9 133.3 %all-to-all-start = ((s32[128,1,1]{2,1,0:T(1,128)}), s32[128,1,1]{2,1,0:T(1,128)S(1)}, u32[]{:S(2)}, u32[]{:S(2)}) async-start(s32[128,1,1]{2,1,0:T(1,128)} %copy.10), calls=%async_computation | async-start | bytes 131072 | tf_op jit(solution)/shard_map/all_to_all | solution.py:39
  30.5 441.3 %all-reduce.5.cloned.1.call-start = ((), (), s32[]{:S(2)}) async-start(), calls=%async_computation.1 | async-start | bytes 1048576
  143.2 678.5 %copy-start = (f32[512]{0:T(512)S(1)}, f32[512]{0:T(512)}, u32[]{:S(2)}) copy-start(f32[512]{0:T(512)} %param.11) | copy-start | bytes 6148
  143.2 678.5 %copy-start.1 = (s32[64]{0:T(128)S(1)}, s32[64]{0:T(128)}, u32[]{:S(2)}) copy-start(s32[64]{0:T(128)} %param.7) | copy-start | bytes 772
  143.2 678.5 %copy-start.2 = (s32[4]{0:T(128)S(1)}, s32[4]{0:T(128)}, u32[]{:S(2)}) copy-start(s32[4]{0:T(128)} %param.10) | copy-start | bytes 52
  147.3 1109.0 %all-reduce.7.cloned.1.call-start = ((), (), s32[]{:S(2)}) async-start(), calls=%async_computation.2 | async-start | bytes 1048576
Sparse Core Ops, SparseCore 0:
  147.4 324.3 all-reduce.4
  932.2 324.0 all-reduce.6
where the time goes:
time: 1720 us
  blocking collectives  988 us (57%)
  waiting for transfers between devices  647 us (38%)
  matrix products  33.5 us (2%)
  starting transfers between devices  20.6 us (1%)
  between operations  18.6 us (1%)
    unnamed x4, waiting for transfers between devices  647 us
    psum x2, blocking collectives, cell_length(): return jnp.sqrt(lax.psum(jnp.sum(vector * vector), 'blk') + epsilon)  501 us
    psum x3, blocking collectives, ray_length(): lax.psum(jnp.sum(vector * vector), ('blk', 'grp')) + epsilon  310 us
    all_gather x2, blocking collectives, body(): model_all = lax.all_gather(model_dir, 'blk', axis=0, tiled=True)  161 us
  transfers between devices with their start and end apart: 3, of which 2 were waited for; matrix products, arithmetic and copies ran while one was open for 0% of the time, Pallas kernels for 0%

commit v1 on v0

v1 whole, which is shorter than its diff:
```python
import jax
import jax.numpy as jnp
from jax import lax
from jax.experimental import pallas as pl
from jax.experimental.pallas import tpu as pltpu
from jax.sharding import PartitionSpec as P

EPS = 1e-06
TILE = 128
NTD = 64
RPD = 4
CPD = 8
NB = 128
NG = 4
NZ = 16
NY = 8
CHUNKS = 4
MESH = pl.DeviceIdType.MESH
F32 = jnp.float32
BF16 = jnp.bfloat16


def pieces(x):
    hi = x.astype(BF16)
    rest = x - hi.astype(F32)
    mid = rest.astype(BF16)
    low = (rest - mid.astype(F32)).astype(BF16)
    return jnp.concatenate([hi, mid, low], axis=0)


def pick(onehot3, x):
    return jnp.dot(onehot3, pieces(x), preferred_element_type=F32)


def kernel(
    jac_hbm, row_hbm, slot_hbm, slotv_hbm, list_hbm, count_hbm, time_hbm,
    sol_ref, ray_ref,
    jac, row_s, slot_s, slot_v, list_v, count_s, time_v,
    ubc, live, part, state,
    send_adj, recv_adj, send_fwd, recv_fwd, send_x, recv_x,
    send_bz, recv_bz, send_bp, recv_bp, send_az, recv_az, send_ay, recv_ay,
    load_sem, small_sem, ssem, rsem,
):
    b = lax.axis_index("blk")
    g = lax.axis_index("grp")
    z, yc = b // NY, b % NY
    y, c = yc // 2, yc % 2

    per = NTD // CHUNKS
    loads = []
    for q in range(CHUNKS):
        cp = pltpu.make_async_copy(
            jac_hbm.at[q * per:(q + 1) * per], jac.at[q * per:(q + 1) * per], load_sem.at[q]
        )
        cp.start()
        loads.append(cp)
    smalls = []
    for q, (src, dst) in enumerate((
        (row_hbm, row_s), (slot_hbm, slot_s), (slotv_hbm, slot_v),
        (list_hbm, list_v), (count_hbm, count_s), (time_hbm, time_v),
    )):
        cp = pltpu.make_async_copy(src, dst, small_sem.at[q])
        cp.start()
        smalls.append(cp)

    def far_z(j):
        return (z + 8 + (1 - 2 * (j % 2)) * ((j + 1) // 2) + NZ) % NZ

    def far_blk(j):
        q = (j % NY) // 2
        yy = (y + 2 + (1 - 2 * (q % 2)) * ((q + 1) // 2) + 4) % 4
        cc = (c + 1 + j) % 2
        return far_z(j // NY) * NY + yy * 2 + cc

    def plane(j):
        i = (yc * NG + g + 1 + j) % (NY * NG)
        return i // NG, i % NG

    bar = pltpu.get_barrier_semaphore()

    def greet_blk(j, carry):
        pl.semaphore_signal(bar, inc=1, device_id=(far_blk(j), g), device_id_type=MESH)
        return carry

    def greet_grp(j, carry):
        pl.semaphore_signal(
            bar, inc=1, device_id=(z * NY + j % NY, (g + 1 + j // NY) % NG), device_id_type=MESH
        )
        return carry

    lax.fori_loop(0, NB - 1, greet_blk, 0)
    lax.fori_loop(0, NY * (NG - 1), greet_grp, 0)

    for cp in smalls:
        cp.wait()
    slot_row = slot_v[...]
    place = jnp.where(lax.broadcasted_iota(jnp.int32, (NB, NTD), 0) == slot_row, 1.0, 0.0)
    place3 = jnp.concatenate([place.astype(BF16)] * 3, axis=1)
    list_row = list_v[...]
    own = jnp.where(lax.broadcasted_iota(jnp.int32, (CPD, NB), 0) == list_row, 1.0, 0.0)
    own3 = jnp.concatenate([own.astype(BF16)] * 3, axis=1)
    serve = jnp.transpose(own)
    serve3 = jnp.concatenate([serve.astype(BF16)] * 3, axis=1)
    state[0] = jnp.zeros((TILE, TILE), F32)
    ray_index = lax.broadcasted_iota(jnp.int32, (TILE, TILE), 0)
    square = jnp.zeros((8, TILE), F32)
    for r in range(RPD):
        mask = jnp.where(ray_index < count_s[r], 1.0, 0.0)
        live[r] = mask
        d = jnp.transpose(jnp.broadcast_to(time_v[r:r + 1, :], (TILE, TILE))) * mask
        ubc[r] = d
        square = square + jnp.sum((d * d).reshape(16, 8, TILE), axis=0)

    def adjoint(lo, hi):
        def one(k, carry):
            prod = jac[k] * ubc[row_s[k]]
            part[k] = jnp.sum(prod.reshape(16, 8, TILE), axis=0)
            return carry
        lax.fori_loop(lo, hi, one, 0, unroll=4)

    def forward(vec):
        def one(k, last):
            r = row_s[k]
            prev = jnp.where(r == 0, last[0], jnp.where(r == 1, last[1], jnp.where(r == 2, last[2], last[3])))
            state[k + 1] = state[prev] + jac[k] * vec[pl.ds(slot_s[k], 1), :]
            return tuple(jnp.where(r == i, k + 1, last[i]) for i in range(RPD))
        zero = jnp.int32(0)
        last = lax.fori_loop(0, NTD, one, (zero,) * RPD, unroll=4)
        return [jnp.sum(state[last[i]], axis=1, keepdims=True) for i in range(RPD)]

    def remote(src, dst, n, device):
        pltpu.make_async_remote_copy(
            src_ref=src, dst_ref=dst, send_sem=ssem.at[n], recv_sem=rsem.at[n],
            device_id=device, device_id_type=MESH,
        ).start()

    def arrived(buf, rows, n):
        pltpu.make_async_copy(buf.at[0:rows], buf.at[0:rows], rsem.at[n]).wait()

    def left(buf, rows, n):
        pltpu.make_async_copy(buf.at[0:rows], buf.at[0:rows], ssem.at[n]).wait()

    def send_rows(src, dst, n):
        def one(j, carry):
            t = far_blk(j)
            remote(src.at[pl.ds(t, 1)], dst.at[pl.ds(b, 1)], n, (t, g))
            return carry
        lax.fori_loop(0, NB - 1, one, 0)

    def send_z(src, dst, n):
        def one(j, carry):
            remote(src.at[0:1], dst.at[pl.ds(z, 1)], n, (far_z(j) * NY + yc, g))
            return carry
        lax.fori_loop(0, NZ - 1, one, 0)

    ADJ, FWD, XCH, BZ, BP, AZ, AY = 0, 2, 4, 6, 9, 12, 14

    def beta_first(i, row):
        send_bz[i, 0:1] = row
        recv_bz[i, pl.ds(z, 1)] = row
        send_z(send_bz.at[i], recv_bz.at[i], BZ + i)

    def beta_second(i):
        arrived(recv_bz.at[i], NZ - 1, BZ + i)
        row = jnp.sum(recv_bz[i], axis=0, keepdims=True)
        send_bp[i, 0:1] = row
        recv_bp[i, pl.ds(yc * NG + g, 1)] = row

        def one(j, carry):
            q, h = plane(j)
            remote(send_bp.at[i, 0:1], recv_bp.at[i, pl.ds(yc * NG + g, 1)], BP + i, (z * NY + q, h))
            return carry
        lax.fori_loop(0, NY * NG - 1, one, 0)

    def beta_last(i):
        arrived(recv_bp.at[i], NY * NG - 1, BP + i)
        return jnp.sqrt(jnp.sum(recv_bp[i], axis=0, keepdims=True) + EPS)

    def alpha_first(i, s):
        row = jnp.sum(s * s, axis=0, keepdims=True)
        send_az[i, 0:1] = row
        recv_az[i, pl.ds(z, 1)] = row
        send_z(send_az.at[i], recv_az.at[i], AZ + i)

    def alpha_second(i):
        arrived(recv_az.at[i], NZ - 1, AZ + i)
        row = jnp.sum(recv_az[i], axis=0, keepdims=True)
        send_ay[i, 0:1] = row
        recv_ay[i, pl.ds(yc, 1)] = row

        def one(j, carry):
            q = (yc + 1 + j) % NY
            remote(send_ay.at[i, 0:1], recv_ay.at[i, pl.ds(yc, 1)], AY + i, (z * NY + q, g))
            return carry
        lax.fori_loop(0, NY - 1, one, 0)

    def alpha_last(i):
        arrived(recv_ay.at[i], NY - 1, AY + i)
        row = jnp.sum(recv_ay[i], axis=0, keepdims=True)
        total = jnp.sum(row, axis=1, keepdims=True)
        return jnp.broadcast_to(jnp.sqrt(total + EPS), (1, TILE))

    def adjoint_pack(i):
        rows = jnp.sum(part[...], axis=1)
        send_adj[i] = pick(place3, rows)

    def adjoint_send(i):
        recv_adj[i, pl.ds(b, 1)] = send_adj[i, pl.ds(b, 1)]
        send_rows(send_adj.at[i], recv_adj.at[i], ADJ + i)

    def adjoint_sum(i):
        arrived(recv_adj.at[i], NB - 1, ADJ + i)
        mine = pick(own3, recv_adj[i])
        send_x[i] = mine
        recv_x[i, pl.ds(g, 1)] = mine[None]

        def one(j, carry):
            h = (g + 1 + j) % NG
            remote(send_x.at[i], recv_x.at[i, g], XCH + i, (b, h))
            return carry
        lax.fori_loop(0, NG - 1, one, 0)

    def adjoint_total(i):
        arrived(recv_x.at[i], NG - 1, XCH + i)
        return jnp.sum(recv_x[i], axis=0)

    def forward_send(i, s):
        alpha_first(i, s)
        send_fwd[i] = pick(serve3, s)
        recv_fwd[i, pl.ds(b, 1)] = send_fwd[i, pl.ds(b, 1)]
        send_rows(send_fwd.at[i], recv_fwd.at[i], FWD + i)

    def forward_sum(i):
        alpha_second(i)
        arrived(recv_fwd.at[i], NB - 1, FWD + i)
        return forward(recv_fwd.at[i])

    def next_ray(sums, by, keep):
        total = jnp.zeros((8, TILE), F32)
        for r in range(RPD):
            t = sums[r] * live[r] * by - keep * ubc[r]
            ubc[r] = t
            total = total + jnp.sum((t * t).reshape(16, 8, TILE), axis=0)
        return jnp.sum(total, axis=0, keepdims=True)

    for q in range(CHUNKS):
        loads[q].wait()
        adjoint(q * per, (q + 1) * per)
    adjoint_pack(0)
    pl.semaphore_wait(bar, NB - 1 + NY * (NG - 1))
    beta_first(0, jnp.sum(square, axis=0, keepdims=True))
    adjoint_send(0)
    beta_second(0)
    adjoint_sum(0)
    beta0 = beta_last(0)
    s0 = adjoint_total(0) / beta0

    forward_send(0, s0)
    sums = forward_sum(0)
    alpha0 = alpha_last(0)
    square1 = next_ray(sums, 1.0 / alpha0, alpha0 / beta0)
    beta_first(1, square1)
    adjoint(0, NTD)
    adjoint_pack(1)
    adjoint_send(1)
    v0 = s0 / alpha0
    beta_second(1)
    adjoint_sum(1)
    beta1 = beta_last(1)
    s1 = adjoint_total(1) / beta1 - beta1 * v0

    forward_send(1, s1)
    rho1 = jnp.sqrt(alpha0 * alpha0 + beta1 * beta1)
    cos1, sin1 = alpha0 / rho1, beta1 / rho1
    sums = forward_sum(1)
    alpha1 = alpha_last(1)
    square2 = next_ray(sums, 1.0 / alpha1, alpha1 / beta1)
    beta_first(2, square2)
    v1 = s1 / alpha1
    theta1 = sin1 * alpha1
    rhobar = -cos1 * alpha1
    phi1 = cos1 * beta0
    phibar = sin1 * beta0
    sol = phi1 / rho1 * v0
    w1 = v1 - theta1 / rho1 * v0
    diagonal = jnp.where(ray_index == lax.broadcasted_iota(jnp.int32, (TILE, TILE), 1), 1.0, 0.0)
    rays = [jnp.sum(ubc[r] * diagonal, axis=0, keepdims=True) for r in range(RPD)]
    beta_second(2)
    beta2 = beta_last(2)
    rho2 = jnp.sqrt(rhobar * rhobar + beta2 * beta2)
    phi2 = rhobar / rho2 * phibar
    sol_ref[...] = sol + phi2 / rho2 * w1
    for r in range(RPD):
        ray_ref[r:r + 1, :] = rays[r] / beta2

    for i in range(2):
        left(send_adj.at[i], NB - 1, ADJ + i)
        left(send_fwd.at[i], NB - 1, FWD + i)
        left(recv_x.at[i], NG - 1, XCH + i)
        left(recv_az.at[i], NZ - 1, AZ + i)
        left(recv_ay.at[i], NY - 1, AY + i)
    for i in range(3):
        left(recv_bz.at[i], NZ - 1, BZ + i)
        left(recv_bp.at[i], NY * NG - 1, BP + i)


def body(jac_tiles, tile_row, tile_slot, send_list, ray_counts, travel_times):
    vmem, smem = pltpu.VMEM, pltpu.SMEM
    scratch = [
        vmem((NTD, TILE, TILE), F32), smem((NTD,), jnp.int32), smem((NTD,), jnp.int32),
        vmem((1, NTD), jnp.int32), vmem((1, NB), jnp.int32), smem((RPD,), jnp.int32),
        vmem((RPD, TILE), F32),
        vmem((RPD, TILE, TILE), F32), vmem((RPD, TILE, TILE), F32),
        vmem((NTD, 8, TILE), F32), vmem((NTD + 1, TILE, TILE), F32),
        vmem((2, NB, TILE), F32), vmem((2, NB, TILE), F32),
        vmem((2, NB, TILE), F32), vmem((2, NB, TILE), F32),
        vmem((2, CPD, TILE), F32), vmem((2, NG, CPD, TILE), F32),
        vmem((3, 8, TILE), F32), vmem((3, NZ, TILE), F32),
        vmem((3, 8, TILE), F32), vmem((3, NY * NG, TILE), F32),
        vmem((2, 8, TILE), F32), vmem((2, NZ, TILE), F32),
        vmem((2, 8, TILE), F32), vmem((2, NY, TILE), F32),
        pltpu.SemaphoreType.DMA((CHUNKS,)), pltpu.SemaphoreType.DMA((6,)),
        pltpu.SemaphoreType.DMA((16,)), pltpu.SemaphoreType.DMA((16,)),
    ]
    sol, ray = pl.pallas_call(
        kernel,
        out_shape=(
            jax.ShapeDtypeStruct((CPD, TILE), F32),
            jax.ShapeDtypeStruct((RPD, TILE), F32),
        ),
        in_specs=[pl.BlockSpec(memory_space=pl.ANY)] * 7,
        out_specs=(pl.BlockSpec(memory_space=vmem),) * 2,
        scratch_shapes=scratch,
        compiler_params=pltpu.CompilerParams(
            collective_id=0, has_side_effects=True, vmem_limit_bytes=56 * 1024 * 1024
        ),
        cost_estimate=pl.CostEstimate(flops=8 * NTD * TILE * TILE, bytes_accessed=4 * NTD * TILE * TILE, transcendentals=0),
    )(
        jac_tiles, tile_row, tile_slot, tile_slot.reshape(1, NTD), send_list.reshape(1, NB),
        ray_counts, travel_times.reshape(RPD, TILE),
    )
    return sol.reshape(-1), ray.reshape(-1)


def solution(mesh):
    spread = P(("blk", "grp"))
    in_specs = (P(("blk", "grp"), None, None),) + (spread,) * 5
    return jax.shard_map(
        body, mesh=mesh, in_specs=in_specs, out_specs=(P("blk"), spread), check_vma=False
    )
```

time: 1720 us -> 87.7 us (0.05)
  blocking collectives: 988 us -> 0 us
  waiting for transfers between devices: 647 us -> 0 us
  Pallas kernels: 0 us -> 84.4 us
  matrix products: 33.5 us -> 0 us
  starting transfers between devices: 20.6 us -> 0 us
  between operations: 18.6 us -> 0.64 us
    psum x7 -> x0, blocking collectives: 827 us -> none  [the longest x2 501 us: cell_length(): return jnp.sqrt(lax.psum(jnp.sum(vector * vector), 'blk') + epsilon)]
    unnamed x4 -> x0, waiting for transfers between devices: 647 us -> none
    all_gather x2 -> x0, blocking collectives: 161 us -> none  [body(): model_all = lax.all_gather(model_dir, 'blk', axis=0, tiled=True)]
    pallas_call x0 -> x1, Pallas kernels: none -> 84.4 us  [body(): pl.pallas_call(kernel, out_shape=(jax.ShapeDtypeStruct((CPD, TILE), F32),...]
    dot_general x12 -> x0, matrix products: 33.5 us -> none  [the longest x2 16.6 us: body(): products = jnp.einsum('kij,kj->ki', jac_tiles, picked, precision=highest)]
    all_to_all x1 -> x0, starting transfers between devices: 20.6 us -> none  [body(): lax.all_to_all(send_list.reshape(blk_count, 1), 'blk', split_axis=0, conc...]
  transfers between devices with their start and end apart: 3 -> 0, of which waited for: 2 -> 0; matrix products, arithmetic and copies ran while one was open for 0% -> 0% of each run, Pallas kernels for 0% -> 0%
where the time goes in v1:
time: 87.7 us; the launch traced here: 87.5 us
  Pallas kernels  84.4 us (96%)
  local copies, waits for them, and re-layouts  2.5 us (3%)
    pallas_call x1, Pallas kernels, body(): pl.pallas_call(kernel, out_shape=(jax.ShapeDtypeStruct((CPD, TILE), F32),...  84.4 us
    unnamed x2, local copies, waits for them, and re-layouts  2.5 us

profile of v1, /device:TPU:1, one launch (start us, length us, event | category | flops | bytes accessed | tf_op | source)
XLA Modules:
  0.0 87.5 jit_solution(13132490268069940890)
XLA Ops:
  0.6 84.4 %shard_map.77 = (f32[8,128]{1,0:T(8,128)}, f32[4,128]{1,0:T(4,128)}) custom-call(f32[64,128,128]{2,1,0:T(8,128)} %jac_hbm.1, s32[64]{0:T(128)} %row_hbm.1, s32[64]{0:T(128)} %slot_hbm.1, s32[1,64]{1,0:T(1,128)} %bitcast.7, s32[1,128]{1,0:T(1,128)} %bitcast.9, s32[4]{0:T(128)} %count_hbm.1, f32[4,128]{1,0:T(4,128)} %bitcast.6), custom_call_target="tpu_custom_call" | custom-call | flops 8388608 | bytes 4194304 | tf_op jit(solution)/shard_map/pallas_call | solution.py:325
  85.0 1.3 %copy.10 = f32[1024]{0:T(1024)} copy(f32[1024]{0:T(1024)} %bitcast.5) | data formatting | bytes 8192
  86.3 1.2 %copy.11 = f32[512]{0:T(512)} copy(f32[512]{0:T(512)} %bitcast.8) | data formatting | bytes 4096

commit v2 on v1

--- a/solution.py
+++ b/solution.py
@@ -34,7 +34,7 @@
 
 def kernel(
     jac_hbm, row_hbm, slot_hbm, slotv_hbm, list_hbm, count_hbm, time_hbm,
-    sol_ref, ray_ref,
+    out_ref,
     jac, row_s, slot_s, slot_v, list_v, count_s, time_v,
     ubc, live, part, state,
     send_adj, recv_adj, send_fwd, recv_fwd, send_x, recv_x,
@@ -44,7 +44,6 @@
     b = lax.axis_index("blk")
     g = lax.axis_index("grp")
     z, yc = b // NY, b % NY
-    y, c = yc // 2, yc % 2
 
     per = NTD // CHUNKS
     loads = []
@@ -67,10 +66,7 @@
         return (z + 8 + (1 - 2 * (j % 2)) * ((j + 1) // 2) + NZ) % NZ
 
     def far_blk(j):
-        q = (j % NY) // 2
-        yy = (y + 2 + (1 - 2 * (q % 2)) * ((q + 1) // 2) + 4) % 4
-        cc = (c + 1 + j) % 2
-        return far_z(j // NY) * NY + yy * 2 + cc
+        return far_z(j // NY) * NY + (yc + 7 * (j % NY) + 7) % NY
 
     def plane(j):
         i = (yc * NG + g + 1 + j) % (NY * NG)
@@ -83,13 +79,11 @@
         return carry
 
     def greet_grp(j, carry):
-        pl.semaphore_signal(
-            bar, inc=1, device_id=(z * NY + j % NY, (g + 1 + j // NY) % NG), device_id_type=MESH
-        )
+        pl.semaphore_signal(bar, inc=1, device_id=(b, (g + 1 + j) % NG), device_id_type=MESH)
         return carry
 
     lax.fori_loop(0, NB - 1, greet_blk, 0)
-    lax.fori_loop(0, NY * (NG - 1), greet_grp, 0)
+    lax.fori_loop(0, NG - 1, greet_grp, 0)
 
     for cp in smalls:
         cp.wait()
@@ -197,8 +191,7 @@
     def alpha_last(i):
         arrived(recv_ay.at[i], NY - 1, AY + i)
         row = jnp.sum(recv_ay[i], axis=0, keepdims=True)
-        total = jnp.sum(row, axis=1, keepdims=True)
-        return jnp.broadcast_to(jnp.sqrt(total + EPS), (1, TILE))
+        return jnp.broadcast_to(jnp.sum(row, axis=1, keepdims=True), (1, TILE))
 
     def adjoint_pack(i):
         rows = jnp.sum(part[...], axis=1)
@@ -247,23 +240,24 @@
         loads[q].wait()
         adjoint(q * per, (q + 1) * per)
     adjoint_pack(0)
-    pl.semaphore_wait(bar, NB - 1 + NY * (NG - 1))
+    pl.semaphore_wait(bar, NB - 1 + NG - 1)
     beta_first(0, jnp.sum(square, axis=0, keepdims=True))
     adjoint_send(0)
+    adjoint_sum(0)
+    raw0 = adjoint_total(0)
+
+    forward_send(0, raw0)
     beta_second(0)
-    adjoint_sum(0)
+    sums = forward_sum(0)
     beta0 = beta_last(0)
-    s0 = adjoint_total(0) / beta0
-
-    forward_send(0, s0)
-    sums = forward_sum(0)
-    alpha0 = alpha_last(0)
-    square1 = next_ray(sums, 1.0 / alpha0, alpha0 / beta0)
+    alpha0 = jnp.sqrt(alpha_last(0) / (beta0 * beta0) + EPS)
+    inverse = 1.0 / (alpha0 * beta0)
+    square1 = next_ray(sums, inverse, alpha0 / beta0)
     beta_first(1, square1)
     adjoint(0, NTD)
     adjoint_pack(1)
     adjoint_send(1)
-    v0 = s0 / alpha0
+    v0 = raw0 * inverse
     beta_second(1)
     adjoint_sum(1)
     beta1 = beta_last(1)
@@ -273,7 +267,7 @@
     rho1 = jnp.sqrt(alpha0 * alpha0 + beta1 * beta1)
     cos1, sin1 = alpha0 / rho1, beta1 / rho1
     sums = forward_sum(1)
-    alpha1 = alpha_last(1)
+    alpha1 = jnp.sqrt(alpha_last(1) + EPS)
     square2 = next_ray(sums, 1.0 / alpha1, alpha1 / beta1)
     beta_first(2, square2)
     v1 = s1 / alpha1
@@ -289,9 +283,9 @@
     beta2 = beta_last(2)
     rho2 = jnp.sqrt(rhobar * rhobar + beta2 * beta2)
     phi2 = rhobar / rho2 * phibar
-    sol_ref[...] = sol + phi2 / rho2 * w1
+    out_ref[0:CPD, :] = sol + phi2 / rho2 * w1
     for r in range(RPD):
-        ray_ref[r:r + 1, :] = rays[r] / beta2
+        out_ref[CPD + r:CPD + r + 1, :] = rays[r] / beta2
 
     for i in range(2):
         left(send_adj.at[i], NB - 1, ADJ + i)
@@ -302,6 +296,11 @@
     for i in range(3):
         left(recv_bz.at[i], NZ - 1, BZ + i)
         left(recv_bp.at[i], NY * NG - 1, BP + i)
+
+
+def split(both_ref, sol_ref, ray_ref):
+    sol_ref[...] = both_ref[:CPD]
+    ray_ref[...] = both_ref[CPD:CPD + RPD]
 
 
 def body(jac_tiles, tile_row, tile_slot, send_list, ray_counts, travel_times):
@@ -322,14 +321,11 @@
         pltpu.SemaphoreType.DMA((CHUNKS,)), pltpu.SemaphoreType.DMA((6,)),
         pltpu.SemaphoreType.DMA((16,)), pltpu.SemaphoreType.DMA((16,)),
     ]
-    sol, ray = pl.pallas_call(
+    both = pl.pallas_call(
         kernel,
-        out_shape=(
-            jax.ShapeDtypeStruct((CPD, TILE), F32),
-            jax.ShapeDtypeStruct((RPD, TILE), F32),
-        ),
+        out_shape=jax.ShapeDtypeStruct((2 * CPD, TILE), F32),
         in_specs=[pl.BlockSpec(memory_space=pl.ANY)] * 7,
-        out_specs=(pl.BlockSpec(memory_space=vmem),) * 2,
+        out_specs=pl.BlockSpec(memory_space=vmem),
         scratch_shapes=scratch,
         compiler_params=pltpu.CompilerParams(
             collective_id=0, has_side_effects=True, vmem_limit_bytes=56 * 1024 * 1024
@@ -339,6 +335,13 @@
         jac_tiles, tile_row, tile_slot, tile_slot.reshape(1, NTD), send_list.reshape(1, NB),
         ray_counts, travel_times.reshape(RPD, TILE),
     )
+    sol, ray = pl.pallas_call(
+        split,
+        out_shape=(
+            jax.ShapeDtypeStruct((CPD, TILE), F32),
+            jax.ShapeDtypeStruct((RPD, TILE), F32),
+        ),
+    )(both)
     return sol.reshape(-1), ray.reshape(-1)
 
 

time: 87.7 us -> 79.6 us (0.908)
  Pallas kernels: 84.4 us -> 78.8 us
  local copies, waits for them, and re-layouts: 2.5 us -> 0 us
    pallas_call x1 -> x2, Pallas kernels: 84.4 us -> 78.8 us  [the longest x1 77.5 us: body(): pl.pallas_call(kernel, out_shape=jax.ShapeDtypeStruct((2 * CPD, TILE), F3...]
    unnamed x2 -> x0, local copies, waits for them, and re-layouts: 2.5 us -> none
where the time goes in v2:
time: 79.6 us; the launch traced here: 79.4 us
  Pallas kernels  78.8 us (99%)
    pallas_call x1, Pallas kernels, body(): pl.pallas_call(kernel, out_shape=jax.ShapeDtypeStruct((2 * CPD, TILE), F3...  77.5 us

profile of v2, /device:TPU:1, one launch (start us, length us, event | category | flops | bytes accessed | tf_op | source)
XLA Modules:
  0.0 79.4 jit_solution(8198864399779874405)
XLA Ops:
  0.6 77.5 %shard_map.77.both_ref = f32[16,128]{1,0:T(8,128)} custom-call(f32[64,128,128]{2,1,0:T(8,128)} %jac_hbm.1, s32[64]{0:T(128)} %row_hbm.1, s32[64]{0:T(128)} %slot_hbm.1, s32[1,64]{1,0:T(1,128)} %bitcast.6, s32[1,128]{1,0:T(1,128)} %bitcast.7, s32[4]{0:T(128)} %count_hbm.1, f32[4,128]{1,0:T(4,128)} %bitcast.5), custom_call_target="tpu_custom_call" | custom-call | flops 8388608 | bytes 4194304 | tf_op jit(solution)/shard_map/pallas_call | solution.py:324
  78.1 1.3 %shard_map.78 = (f32[8,128]{1,0:T(8,128)}, f32[4,128]{1,0:T(4,128)}) custom-call(f32[16,128]{1,0:T(8,128)} %shard_map.77.both_ref), custom_call_target="tpu_custom_call" | custom-call | tf_op jit(solution)/shard_map/pallas_call | solution.py:338

commit v3 on v2

--- a/solution.py
+++ b/solution.py
@@ -36,14 +36,37 @@
     jac_hbm, row_hbm, slot_hbm, slotv_hbm, list_hbm, count_hbm, time_hbm,
     out_ref,
     jac, row_s, slot_s, slot_v, list_v, count_s, time_v,
-    ubc, live, part, state,
+    ubc, fbc, live, part, state,
     send_adj, recv_adj, send_fwd, recv_fwd, send_x, recv_x,
     send_bz, recv_bz, send_bp, recv_bp, send_az, recv_az, send_ay, recv_ay,
+    send_end, recv_end, send_eg, recv_eg,
     load_sem, small_sem, ssem, rsem,
 ):
     b = lax.axis_index("blk")
     g = lax.axis_index("grp")
     z, yc = b // NY, b % NY
+
+    def far_z(j):
+        return (z + 8 + (1 - 2 * (j % 2)) * ((j + 1) // 2) + NZ) % NZ
+
+    def far_blk(j):
+        return far_z(j // NY) * NY + (yc + 7 * (j % NY) + 7) % NY
+
+    def plane(j):
+        i = (yc * NG + g + 1 + j) % (NY * NG)
+        return i // NG, i % NG
+
+    bar = pltpu.get_barrier_semaphore()
+
+    def greet_blk(j, carry):
+        pl.semaphore_signal(bar, inc=1, device_id=(far_blk(j), g), device_id_type=MESH)
+        return carry
+
+    def greet_grp(j, carry):
+        pl.semaphore_signal(bar, inc=1, device_id=(b, (g + 1 + j) % NG), device_id_type=MESH)
+        return carry
+
+    lax.fori_loop(0, NB // 2, greet_blk, 0)
 
     per = NTD // CHUNKS
     loads = []
@@ -62,27 +85,7 @@
         cp.start()
         smalls.append(cp)
 
-    def far_z(j):
-        return (z + 8 + (1 - 2 * (j % 2)) * ((j + 1) // 2) + NZ) % NZ
-
-    def far_blk(j):
-        return far_z(j // NY) * NY + (yc + 7 * (j % NY) + 7) % NY
-
-    def plane(j):
-        i = (yc * NG + g + 1 + j) % (NY * NG)
-        return i // NG, i % NG
-
-    bar = pltpu.get_barrier_semaphore()
-
-    def greet_blk(j, carry):
-        pl.semaphore_signal(bar, inc=1, device_id=(far_blk(j), g), device_id_type=MESH)
-        return carry
-
-    def greet_grp(j, carry):
-        pl.semaphore_signal(bar, inc=1, device_id=(b, (g + 1 + j) % NG), device_id_type=MESH)
-        return carry
-
-    lax.fori_loop(0, NB - 1, greet_blk, 0)
+    lax.fori_loop(NB // 2, NB - 1, greet_blk, 0)
     lax.fori_loop(0, NG - 1, greet_grp, 0)
 
     for cp in smalls:
@@ -105,9 +108,9 @@
         ubc[r] = d
         square = square + jnp.sum((d * d).reshape(16, 8, TILE), axis=0)
 
-    def adjoint(lo, hi):
+    def adjoint(lo, hi, src):
         def one(k, carry):
-            prod = jac[k] * ubc[row_s[k]]
+            prod = jac[k] * src[row_s[k]]
             part[k] = jnp.sum(prod.reshape(16, 8, TILE), axis=0)
             return carry
         lax.fori_loop(lo, hi, one, 0, unroll=4)
@@ -147,7 +150,7 @@
             return carry
         lax.fori_loop(0, NZ - 1, one, 0)
 
-    ADJ, FWD, XCH, BZ, BP, AZ, AY = 0, 2, 4, 6, 9, 12, 14
+    ADJ, FWD, XCH, BZ, BP, AZ, AY, END = 0, 2, 4, 6, 8, 10, 12, 14
 
     def beta_first(i, row):
         send_bz[i, 0:1] = row
@@ -168,7 +171,39 @@
 
     def beta_last(i):
         arrived(recv_bp.at[i], NY * NG - 1, BP + i)
-        return jnp.sqrt(jnp.sum(recv_bp[i], axis=0, keepdims=True) + EPS)
+        return jnp.sum(recv_bp[i], axis=0, keepdims=True)
+
+    def final_first(row):
+        send_end[0:1] = row
+        recv_end[pl.ds(b, 1)] = row
+
+        def one(j, carry):
+            remote(send_end.at[0:1], recv_end.at[pl.ds(b, 1)], END, (far_blk(j), g))
+            return carry
+        lax.fori_loop(0, NB - 1, one, 0)
+
+    def final_norm():
+        arrived(recv_end, NB - 1, END)
+        total = jnp.sum(recv_end[...], axis=0, keepdims=True)
+        send_eg[0:1] = total
+        recv_eg[pl.ds(g, 1)] = total
+
+        def one(j, carry):
+            remote(send_eg.at[0:1], recv_eg.at[pl.ds(g, 1)], END + 1, (b, (g + 1 + j) % NG))
+            return carry
+        lax.fori_loop(0, NG - 1, one, 0)
+        arrived(recv_eg, NG - 1, END + 1)
+        return jnp.sqrt(jnp.sum(recv_eg[0:NG], axis=0, keepdims=True) + EPS)
+
+    def early_out():
+        for i in range(2):
+            left(send_adj.at[i], NB - 1, ADJ + i)
+            left(send_fwd.at[i], NB - 1, FWD + i)
+            left(recv_x.at[i], NG - 1, XCH + i)
+            left(recv_az.at[i], NZ - 1, AZ + i)
+            left(recv_ay.at[i], NY - 1, AY + i)
+            left(recv_bz.at[i], NZ - 1, BZ + i)
+            left(recv_bp.at[i], NY * NG - 1, BP + i)
 
     def alpha_first(i, s):
         row = jnp.sum(s * s, axis=0, keepdims=True)
@@ -238,7 +273,7 @@
 
     for q in range(CHUNKS):
         loads[q].wait()
-        adjoint(q * per, (q + 1) * per)
+        adjoint(q * per, (q + 1) * per, ubc)
     adjoint_pack(0)
     pl.semaphore_wait(bar, NB - 1 + NG - 1)
     beta_first(0, jnp.sum(square, axis=0, keepdims=True))
@@ -249,19 +284,37 @@
     forward_send(0, raw0)
     beta_second(0)
     sums = forward_sum(0)
-    beta0 = beta_last(0)
-    alpha0 = jnp.sqrt(alpha_last(0) / (beta0 * beta0) + EPS)
-    inverse = 1.0 / (alpha0 * beta0)
-    square1 = next_ray(sums, inverse, alpha0 / beta0)
-    beta_first(1, square1)
-    adjoint(0, NTD)
+    lane = lax.broadcasted_iota(jnp.int32, (1, TILE), 1)
+    ff = jnp.zeros((8, TILE), F32)
+    fd = jnp.zeros((8, TILE), F32)
+    for r in range(RPD):
+        f = sums[r] * live[r]
+        fbc[r] = f
+        ff = ff + jnp.sum((f * f).reshape(16, 8, TILE), axis=0)
+        fd = fd + jnp.sum((f * ubc[r]).reshape(16, 8, TILE), axis=0)
+    inner = jnp.where(lane < TILE // 2, jnp.sum(ff, axis=0, keepdims=True), jnp.sum(fd, axis=0, keepdims=True))
+    beta_first(1, inner)
+    adjoint(0, NTD, fbc)
     adjoint_pack(1)
     adjoint_send(1)
+    data_square = beta_last(0)
+    beta0_square = data_square + EPS
+    beta0 = jnp.sqrt(beta0_square)
+    alpha0 = jnp.sqrt(alpha_last(0) / beta0_square + EPS)
+    inverse = 1.0 / (alpha0 * beta0)
+    ratio = alpha0 / beta0
+    for r in range(RPD):
+        ubc[r] = fbc[r] * inverse - ratio * ubc[r]
     v0 = raw0 * inverse
     beta_second(1)
     adjoint_sum(1)
-    beta1 = beta_last(1)
-    s1 = adjoint_total(1) / beta1 - beta1 * v0
+    raw1 = adjoint_total(1) * inverse - ratio * raw0
+    inner = beta_last(1)
+    ff = jnp.broadcast_to(jnp.sum(jnp.where(lane == 0, inner, 0.0), axis=1, keepdims=True), (1, TILE))
+    fd = jnp.broadcast_to(jnp.sum(jnp.where(lane == TILE - 1, inner, 0.0), axis=1, keepdims=True), (1, TILE))
+    square1 = (ff * inverse - 2.0 * ratio * fd) * inverse + ratio * ratio * data_square
+    beta1 = jnp.sqrt(jnp.maximum(square1, 0.0) + EPS)
+    s1 = raw1 / beta1 - beta1 * v0
 
     forward_send(1, s1)
     rho1 = jnp.sqrt(alpha0 * alpha0 + beta1 * beta1)
@@ -269,7 +322,7 @@
     sums = forward_sum(1)
     alpha1 = jnp.sqrt(alpha_last(1) + EPS)
     square2 = next_ray(sums, 1.0 / alpha1, alpha1 / beta1)
-    beta_first(2, square2)
+    final_first(square2)
     v1 = s1 / alpha1
     theta1 = sin1 * alpha1
     rhobar = -cos1 * alpha1
@@ -279,23 +332,16 @@
     w1 = v1 - theta1 / rho1 * v0
     diagonal = jnp.where(ray_index == lax.broadcasted_iota(jnp.int32, (TILE, TILE), 1), 1.0, 0.0)
     rays = [jnp.sum(ubc[r] * diagonal, axis=0, keepdims=True) for r in range(RPD)]
-    beta_second(2)
-    beta2 = beta_last(2)
+    early_out()
+    beta2 = final_norm()
     rho2 = jnp.sqrt(rhobar * rhobar + beta2 * beta2)
     phi2 = rhobar / rho2 * phibar
     out_ref[0:CPD, :] = sol + phi2 / rho2 * w1
     for r in range(RPD):
         out_ref[CPD + r:CPD + r + 1, :] = rays[r] / beta2
 
-    for i in range(2):
-        left(send_adj.at[i], NB - 1, ADJ + i)
-        left(send_fwd.at[i], NB - 1, FWD + i)
-        left(recv_x.at[i], NG - 1, XCH + i)
-        left(recv_az.at[i], NZ - 1, AZ + i)
-        left(recv_ay.at[i], NY - 1, AY + i)
-    for i in range(3):
-        left(recv_bz.at[i], NZ - 1, BZ + i)
-        left(recv_bp.at[i], NY * NG - 1, BP + i)
+    left(recv_end, NB - 1, END)
+    left(recv_eg, NG - 1, END + 1)
 
 
 def split(both_ref, sol_ref, ray_ref):
@@ -309,15 +355,16 @@
         vmem((NTD, TILE, TILE), F32), smem((NTD,), jnp.int32), smem((NTD,), jnp.int32),
         vmem((1, NTD), jnp.int32), vmem((1, NB), jnp.int32), smem((RPD,), jnp.int32),
         vmem((RPD, TILE), F32),
-        vmem((RPD, TILE, TILE), F32), vmem((RPD, TILE, TILE), F32),
+        vmem((RPD, TILE, TILE), F32), vmem((RPD, TILE, TILE), F32), vmem((RPD, TILE, TILE), F32),
         vmem((NTD, 8, TILE), F32), vmem((NTD + 1, TILE, TILE), F32),
         vmem((2, NB, TILE), F32), vmem((2, NB, TILE), F32),
         vmem((2, NB, TILE), F32), vmem((2, NB, TILE), F32),
         vmem((2, CPD, TILE), F32), vmem((2, NG, CPD, TILE), F32),
-        vmem((3, 8, TILE), F32), vmem((3, NZ, TILE), F32),
-        vmem((3, 8, TILE), F32), vmem((3, NY * NG, TILE), F32),
+        vmem((2, 8, TILE), F32), vmem((2, NZ, TILE), F32),
+        vmem((2, 8, TILE), F32), vmem((2, NY * NG, TILE), F32),
         vmem((2, 8, TILE), F32), vmem((2, NZ, TILE), F32),
         vmem((2, 8, TILE), F32), vmem((2, NY, TILE), F32),
+        vmem((8, TILE), F32), vmem((NB, TILE), F32), vmem((8, TILE), F32), vmem((8, TILE), F32),
         pltpu.SemaphoreType.DMA((CHUNKS,)), pltpu.SemaphoreType.DMA((6,)),
         pltpu.SemaphoreType.DMA((16,)), pltpu.SemaphoreType.DMA((16,)),
     ]

time: 79.6 us -> 78.2 us (0.982)
  Pallas kernels: 78.8 us -> 77.4 us
    pallas_call x1, Pallas kernels: 77.5 us -> 76.1 us  [body(): pl.pallas_call(kernel, out_shape=jax.ShapeDtypeStruct((2 * CPD, TILE), F3...]
where the time goes in v3:
time: 78.2 us; the launch traced here: 78.1 us
  Pallas kernels  77.4 us (99%)
    pallas_call x1, Pallas kernels, body(): pl.pallas_call(kernel, out_shape=jax.ShapeDtypeStruct((2 * CPD, TILE), F3...  76.1 us

profile of v3, /device:TPU:1, one launch (start us, length us, event | category | flops | bytes accessed | tf_op | source)
XLA Modules:
  0.0 78.1 jit_solution(16978779994812062711)
XLA Ops:
  0.6 76.1 %shard_map.77.both_ref = f32[16,128]{1,0:T(8,128)} custom-call(f32[64,128,128]{2,1,0:T(8,128)} %jac_hbm.1, s32[64]{0:T(128)} %row_hbm.1, s32[64]{0:T(128)} %slot_hbm.1, s32[1,64]{1,0:T(1,128)} %bitcast.6, s32[1,128]{1,0:T(1,128)} %bitcast.7, s32[4]{0:T(128)} %count_hbm.1, f32[4,128]{1,0:T(4,128)} %bitcast.5), custom_call_target="tpu_custom_call" | custom-call | flops 8388608 | bytes 4194304 | tf_op jit(solution)/shard_map/pallas_call | solution.py:371
  76.8 1.3 %shard_map.78 = (f32[8,128]{1,0:T(8,128)}, f32[4,128]{1,0:T(4,128)}) custom-call(f32[16,128]{1,0:T(8,128)} %shard_map.77.both_ref), custom_call_target="tpu_custom_call" | custom-call | tf_op jit(solution)/shard_map/pallas_call | solution.py:385

commit v4 on v3

--- a/solution.py
+++ b/solution.py
@@ -58,15 +58,17 @@
 
     bar = pltpu.get_barrier_semaphore()
 
-    def greet_blk(j, carry):
-        pl.semaphore_signal(bar, inc=1, device_id=(far_blk(j), g), device_id_type=MESH)
+    def greet_plane(k, carry):
+        base = far_z(k) * NY
+        for q in range(NY):
+            pl.semaphore_signal(bar, inc=1, device_id=(base + q, g), device_id_type=MESH)
         return carry
 
     def greet_grp(j, carry):
         pl.semaphore_signal(bar, inc=1, device_id=(b, (g + 1 + j) % NG), device_id_type=MESH)
         return carry
 
-    lax.fori_loop(0, NB // 2, greet_blk, 0)
+    lax.fori_loop(0, NZ // 2, greet_plane, 0)
 
     per = NTD // CHUNKS
     loads = []
@@ -85,7 +87,9 @@
         cp.start()
         smalls.append(cp)
 
-    lax.fori_loop(NB // 2, NB - 1, greet_blk, 0)
+    lax.fori_loop(NZ // 2, NZ - 1, greet_plane, 0)
+    for q in range(1, NY):
+        pl.semaphore_signal(bar, inc=1, device_id=(z * NY + (yc + q) % NY, g), device_id_type=MESH)
     lax.fori_loop(0, NG - 1, greet_grp, 0)
 
     for cp in smalls:
@@ -113,7 +117,7 @@
             prod = jac[k] * src[row_s[k]]
             part[k] = jnp.sum(prod.reshape(16, 8, TILE), axis=0)
             return carry
-        lax.fori_loop(lo, hi, one, 0, unroll=4)
+        lax.fori_loop(lo, hi, one, 0, unroll=16)
 
     def forward(vec):
         def one(k, last):
@@ -122,7 +126,7 @@
             state[k + 1] = state[prev] + jac[k] * vec[pl.ds(slot_s[k], 1), :]
             return tuple(jnp.where(r == i, k + 1, last[i]) for i in range(RPD))
         zero = jnp.int32(0)
-        last = lax.fori_loop(0, NTD, one, (zero,) * RPD, unroll=4)
+        last = lax.fori_loop(0, NTD, one, (zero,) * RPD, unroll=16)
         return [jnp.sum(state[last[i]], axis=1, keepdims=True) for i in range(RPD)]
 
     def remote(src, dst, n, device):
@@ -193,7 +197,7 @@
             return carry
         lax.fori_loop(0, NG - 1, one, 0)
         arrived(recv_eg, NG - 1, END + 1)
-        return jnp.sqrt(jnp.sum(recv_eg[0:NG], axis=0, keepdims=True) + EPS)
+        return jnp.sum(recv_eg[0:NG], axis=0, keepdims=True)
 
     def early_out():
         for i in range(2):
@@ -243,7 +247,7 @@
         recv_x[i, pl.ds(g, 1)] = mine[None]
 
         def one(j, carry):
-            h = (g + 1 + j) % NG
+            h = (g + 2 + j + j // 2) % NG
             remote(send_x.at[i], recv_x.at[i, g], XCH + i, (b, h))
             return carry
         lax.fori_loop(0, NG - 1, one, 0)
@@ -263,21 +267,13 @@
         arrived(recv_fwd.at[i], NB - 1, FWD + i)
         return forward(recv_fwd.at[i])
 
-    def next_ray(sums, by, keep):
-        total = jnp.zeros((8, TILE), F32)
-        for r in range(RPD):
-            t = sums[r] * live[r] * by - keep * ubc[r]
-            ubc[r] = t
-            total = total + jnp.sum((t * t).reshape(16, 8, TILE), axis=0)
-        return jnp.sum(total, axis=0, keepdims=True)
-
     for q in range(CHUNKS):
         loads[q].wait()
         adjoint(q * per, (q + 1) * per, ubc)
     adjoint_pack(0)
     pl.semaphore_wait(bar, NB - 1 + NG - 1)
+    adjoint_send(0)
     beta_first(0, jnp.sum(square, axis=0, keepdims=True))
-    adjoint_send(0)
     adjoint_sum(0)
     raw0 = adjoint_total(0)
 
@@ -320,9 +316,19 @@
     rho1 = jnp.sqrt(alpha0 * alpha0 + beta1 * beta1)
     cos1, sin1 = alpha0 / rho1, beta1 / rho1
     sums = forward_sum(1)
+    gg = jnp.zeros((8, TILE), F32)
+    gt = jnp.zeros((8, TILE), F32)
+    tt = jnp.zeros((8, TILE), F32)
+    for r in range(RPD):
+        f = sums[r] * live[r]
+        t = ubc[r]
+        fbc[r] = f
+        gg = gg + jnp.sum((f * f).reshape(16, 8, TILE), axis=0)
+        gt = gt + jnp.sum((f * t).reshape(16, 8, TILE), axis=0)
+        tt = tt + jnp.sum((t * t).reshape(16, 8, TILE), axis=0)
+    gg, gt, tt = (jnp.sum(v, axis=0, keepdims=True) for v in (gg, gt, tt))
+    final_first(jnp.where(lane < 32, gg, jnp.where(lane < 64, gt, tt)))
     alpha1 = jnp.sqrt(alpha_last(1) + EPS)
-    square2 = next_ray(sums, 1.0 / alpha1, alpha1 / beta1)
-    final_first(square2)
     v1 = s1 / alpha1
     theta1 = sin1 * alpha1
     rhobar = -cos1 * alpha1
@@ -330,10 +336,19 @@
     phibar = sin1 * beta0
     sol = phi1 / rho1 * v0
     w1 = v1 - theta1 / rho1 * v0
+    step = alpha1 / beta1
     diagonal = jnp.where(ray_index == lax.broadcasted_iota(jnp.int32, (TILE, TILE), 1), 1.0, 0.0)
-    rays = [jnp.sum(ubc[r] * diagonal, axis=0, keepdims=True) for r in range(RPD)]
+    rays = [
+        jnp.sum((fbc[r] / alpha1 - step * ubc[r]) * diagonal, axis=0, keepdims=True) for r in range(RPD)
+    ]
     early_out()
-    beta2 = final_norm()
+    inner = final_norm()
+    gg, gt, tt = (
+        jnp.broadcast_to(jnp.sum(jnp.where(lane == at, inner, 0.0), axis=1, keepdims=True), (1, TILE))
+        for at in (0, 32, 64)
+    )
+    square2 = (gg / alpha1 - 2.0 * step * gt) / alpha1 + step * step * tt
+    beta2 = jnp.sqrt(jnp.maximum(square2, 0.0) + EPS)
     rho2 = jnp.sqrt(rhobar * rhobar + beta2 * beta2)
     phi2 = rhobar / rho2 * phibar
     out_ref[0:CPD, :] = sol + phi2 / rho2 * w1

time: 78.2 us -> 76.5 us (0.978)
  Pallas kernels: 77.4 us -> 75.6 us
    pallas_call x1, Pallas kernels: 76.1 us -> 74.3 us  [body(): pl.pallas_call(kernel, out_shape=jax.ShapeDtypeStruct((2 * CPD, TILE), F3...]
where the time goes in v4:
time: 76.5 us; the launch traced here: 76.2 us
  Pallas kernels  75.6 us (99%)
    pallas_call x1, Pallas kernels, body(): pl.pallas_call(kernel, out_shape=jax.ShapeDtypeStruct((2 * CPD, TILE), F3...  74.3 us

profile of v4, /device:TPU:1, one launch (start us, length us, event | category | flops | bytes accessed | tf_op | source)
XLA Modules:
  0.0 76.2 jit_solution(14507841439951524918)
XLA Ops:
  0.6 74.3 %shard_map.77.both_ref = f32[16,128]{1,0:T(8,128)} custom-call(f32[64,128,128]{2,1,0:T(8,128)} %jac_hbm.1, s32[64]{0:T(128)} %row_hbm.1, s32[64]{0:T(128)} %slot_hbm.1, s32[1,64]{1,0:T(1,128)} %bitcast.6, s32[1,128]{1,0:T(1,128)} %bitcast.7, s32[4]{0:T(128)} %count_hbm.1, f32[4,128]{1,0:T(4,128)} %bitcast.5), custom_call_target="tpu_custom_call" | custom-call | flops 8388608 | bytes 4194304 | tf_op jit(solution)/shard_map/pallas_call | solution.py:386
  75.0 1.3 %shard_map.78 = (f32[8,128]{1,0:T(8,128)}, f32[4,128]{1,0:T(4,128)}) custom-call(f32[16,128]{1,0:T(8,128)} %shard_map.77.both_ref), custom_call_target="tpu_custom_call" | custom-call | tf_op jit(solution)/shard_map/pallas_call | solution.py:400

commit v5 on v4

--- a/solution.py
+++ b/solution.py
@@ -117,7 +117,7 @@
             prod = jac[k] * src[row_s[k]]
             part[k] = jnp.sum(prod.reshape(16, 8, TILE), axis=0)
             return carry
-        lax.fori_loop(lo, hi, one, 0, unroll=16)
+        lax.fori_loop(lo, hi, one, 0, unroll=32)
 
     def forward(vec):
         def one(k, last):
@@ -126,7 +126,7 @@
             state[k + 1] = state[prev] + jac[k] * vec[pl.ds(slot_s[k], 1), :]
             return tuple(jnp.where(r == i, k + 1, last[i]) for i in range(RPD))
         zero = jnp.int32(0)
-        last = lax.fori_loop(0, NTD, one, (zero,) * RPD, unroll=16)
+        last = lax.fori_loop(0, NTD, one, (zero,) * RPD, unroll=32)
         return [jnp.sum(state[last[i]], axis=1, keepdims=True) for i in range(RPD)]
 
     def remote(src, dst, n, device):
@@ -193,7 +193,7 @@
         recv_eg[pl.ds(g, 1)] = total
 
         def one(j, carry):
-            remote(send_eg.at[0:1], recv_eg.at[pl.ds(g, 1)], END + 1, (b, (g + 1 + j) % NG))
+            remote(send_eg.at[0:1], recv_eg.at[pl.ds(g, 1)], END + 1, (b, (g + 2 + j + j // 2) % NG))
             return carry
         lax.fori_loop(0, NG - 1, one, 0)
         arrived(recv_eg, NG - 1, END + 1)

time: 76.5 us -> 76.5 us (level)
  no operation moved by 1% of the time
where the time goes in v5:
time: 76.5 us; the launch traced here: 76.2 us
  Pallas kernels  75.6 us (99%)
    pallas_call x1, Pallas kernels, body(): pl.pallas_call(kernel, out_shape=jax.ShapeDtypeStruct((2 * CPD, TILE), F3...  74.3 us

profile of v5, /device:TPU:1, one launch (start us, length us, event | category | flops | bytes accessed | tf_op | source)
XLA Modules:
  0.0 76.2 jit_solution(16060461894497570205)
XLA Ops:
  0.6 74.3 %shard_map.77.both_ref = f32[16,128]{1,0:T(8,128)} custom-call(f32[64,128,128]{2,1,0:T(8,128)} %jac_hbm.1, s32[64]{0:T(128)} %row_hbm.1, s32[64]{0:T(128)} %slot_hbm.1, s32[1,64]{1,0:T(1,128)} %bitcast.6, s32[1,128]{1,0:T(1,128)} %bitcast.7, s32[4]{0:T(128)} %count_hbm.1, f32[4,128]{1,0:T(4,128)} %bitcast.5), custom_call_target="tpu_custom_call" | custom-call | flops 8388608 | bytes 4194304 | tf_op jit(solution)/shard_map/pallas_call | solution.py:386
  74.9 1.3 %shard_map.78 = (f32[8,128]{1,0:T(8,128)}, f32[4,128]{1,0:T(4,128)}) custom-call(f32[16,128]{1,0:T(8,128)} %shard_map.77.both_ref), custom_call_target="tpu_custom_call" | custom-call | tf_op jit(solution)/shard_map/pallas_call | solution.py:400
